TPU v7x, 512 devices: a whole 4x4x16 slice. The times are simulated.
512 devices in a mesh: tm: 32 (over y, x, z_hi), zone: 16 (over z_lo, core).
Axes of the slice: x: 4, y: 4, z: 16 (z_hi: 2, z_lo: 8; z = z_hi * 8 + z_lo), core: 2. Of those that a mesh axis runs over, the one named last changes fastest.
Arguments:
- states: bfloat16 [128, 2048, 512], P('tm', 'zone'), may hold values from -6 to 6
- gain_attn: float32 [512], replicated, may hold values from 0.1 to 1.9
- w_qkv: bfloat16 [512, 1536], P('zone')
- w_out_attn: bfloat16 [512, 512], P('zone'), may hold values from -0.25 to 0.25
- pattern: int32 [32, 2], P('tm'), may hold values from 0 to 1, as said below
- gain_mix: float32 [512], replicated, may hold values from 0.1 to 1.9
- neighbours: int32 [16, 3], replicated, may hold values from 0 to 15, as said below
- degree: int32 [16], replicated, may hold values from 1 to 3
- mix: bfloat16 [16, 3, 128, 128], replicated, may hold values from -0.3125 to 0.3125
- gain_ffn: float32 [512], replicated, may hold values from 0.1 to 1.9
- w_in: bfloat16 [512, 2048], P('zone'), may hold values from -0.25 to 0.25
- w_out: bfloat16 [2048, 512], P('zone'), may hold values from -0.125 to 0.125
Outputs:
- evolved: bfloat16 [128, 2048, 512], P('tm', 'zone')
Inputs may be any that keep to these rules, and one draw needn't show every extreme that they name: `pattern`: time blocks 1 to 2 each attend to time block 0. `neighbours`: each row names 3 different zone blocks.
All inputs are finite; a program needn't handle non-finite values.
Results may differ from a plain program's by a relative error of at most 0.008.
Values may be sent and summed in bfloat16 or wider, within the bound.
A program may use at most 64 MiB of HBM per device.

v0:
```python
import jax
import jax.numpy as jnp
from jax import lax
from jax.sharding import PartitionSpec as P

HEADS = 4


def shifted(value, axis, steps):
    count = lax.axis_size(axis)
    first, last = (max(0, -steps), min(count, count - steps))
    return lax.ppermute(value, axis, [(source, source + steps) for source in range(first, last)])


def rms_scale(values, gain):
    mean_sq = jnp.mean(values * values, axis=-1, keepdims=True)
    return values * lax.rsqrt(mean_sq + 1e-06) * gain


def on_device(
    states,
    gain_attn,
    w_qkv,
    w_out_attn,
    pattern,
    gain_mix,
    neighbours,
    degree,
    mix,
    gain_ffn,
    w_in,
    w_out,
):
    steps, zone_rows, width = states.shape
    head_size = width // HEADS
    reach = pattern.shape[1]
    full_qkv, full_attn, full_in, full_out = (
        lax.all_gather(w_qkv, "zone", axis=0, tiled=True),
        lax.all_gather(w_out_attn, "zone", axis=0, tiled=True),
        lax.all_gather(w_in, "zone", axis=0, tiled=True),
        lax.all_gather(w_out, "zone", axis=0, tiled=True),
    )
    input_wide = states.astype(jnp.float32)
    normed = rms_scale(input_wide, gain_attn).astype(jnp.bfloat16)
    projected = jnp.dot(
        normed.reshape(-1, width), full_qkv, preferred_element_type=jnp.float32
    ).astype(jnp.bfloat16)
    projected = projected.reshape(steps, zone_rows, 3 * width)
    queries = projected[..., :width].reshape(steps, zone_rows, HEADS, head_size)
    own_pairs = projected[..., width:]
    earlier = []
    for offset in range(reach, 0, -1):
        earlier.append(shifted(own_pairs, "tm", offset))
    all_pairs = jnp.concatenate(earlier + [own_pairs], axis=0)
    key_count = all_pairs.shape[0]
    keys_all = all_pairs[..., :width].reshape(key_count, zone_rows, HEADS, head_size)
    values_all = all_pairs[..., width:].reshape(key_count, zone_rows, HEADS, head_size)
    scores = jnp.einsum(
        "tzhd,szhd->zhts", queries, keys_all, preferred_element_type=jnp.float32
    ) * head_size ** (-0.5)
    my_block = lax.axis_index("tm")
    key_index = jnp.arange(key_count, dtype=jnp.int32)
    back = reach - key_index // steps
    pattern_row = jnp.concatenate([jnp.ones((1,), jnp.int32), pattern[0]])
    live_back = jnp.sum(
        jnp.where(
            back[:, None] == jnp.arange(reach + 1, dtype=jnp.int32)[None, :],
            pattern_row[None, :],
            0,
        ),
        axis=1,
    )
    query_pos = jnp.arange(steps, dtype=jnp.int32)
    local_key = key_index - reach * steps
    earlier_ok = (back > 0) & (live_back == 1) & (my_block - back >= 0)
    allowed = earlier_ok[None, :] | (back[None, :] == 0) & (
        local_key[None, :] <= query_pos[:, None]
    )
    masked = jnp.where(allowed, scores, -1e30)
    top = jnp.max(masked, axis=-1, keepdims=True)
    expw = jnp.where(allowed, jnp.exp(masked - top), 0.0)
    total = jnp.sum(expw, axis=-1)
    probs = expw.astype(jnp.bfloat16)
    context = jnp.einsum("zhts,szhd->tzhd", probs, values_all, preferred_element_type=jnp.float32)
    context = (
        (context / jnp.transpose(total, (2, 0, 1))[..., None])
        .astype(jnp.bfloat16)
        .reshape(-1, width)
    )
    after_attn = input_wide + jnp.dot(
        context, full_attn, preferred_element_type=jnp.float32
    ).reshape(steps, zone_rows, width)
    mixin = jnp.transpose(rms_scale(after_attn, gain_mix).astype(jnp.bfloat16), (0, 2, 1))
    slot_live = jnp.arange(mix.shape[1], dtype=jnp.int32)[None, :] < degree[:, None]
    live_mix = jnp.where(slot_live[:, :, None, None], mix, jnp.zeros_like(mix))
    items = lax.all_to_all(mixin, "zone", split_axis=1, concat_axis=2, tiled=True)
    count, channels, zones_all = items.shape
    block_count = neighbours.shape[0]
    grid = items.reshape(count, channels, block_count, zones_all // block_count)
    nearby = grid[:, :, neighbours, :]
    spatial = jnp.einsum("ncbky,bkzy->ncbz", nearby, live_mix, preferred_element_type=jnp.float32)
    spatial = spatial.astype(jnp.bfloat16).reshape(count, channels, zones_all)
    returned = lax.all_to_all(spatial, "zone", split_axis=2, concat_axis=1, tiled=True)
    after_mix = after_attn + jnp.transpose(returned, (0, 2, 1)).astype(jnp.float32)
    ffn_in = rms_scale(after_mix, gain_ffn).astype(jnp.bfloat16).reshape(-1, width)
    hidden = jax.nn.gelu(
        jnp.dot(ffn_in, full_in, preferred_element_type=jnp.float32), approximate=True
    ).astype(jnp.bfloat16)
    evolved = after_mix + jnp.dot(hidden, full_out, preferred_element_type=jnp.float32).reshape(
        steps, zone_rows, width
    )
    return evolved.astype(jnp.bfloat16)


def solution(mesh):
    return jax.shard_map(
        on_device,
        mesh=mesh,
        in_specs=(
            P("tm", "zone", None),
            P(),
            P("zone", None),
            P("zone", None),
            P("tm", None),
            P(),
            P(),
            P(),
            P(),
            P(),
            P("zone", None),
            P("zone", None),
        ),
        out_specs=P("tm", "zone", None),
        check_vma=False,
    )
```

profile of v0, /device:TPU:1, one launch (start us, length us, event | category | flops | bytes accessed | tf_op | source)
XLA Modules:
  0.0 382.1 jit_solution(14407234201258981439)
XLA Ops:
  6.5 0.7 all-gather.4.cloned.1.call-update
  7.3 0.7 all-gather.6.cloned.1.call-update
  8.0 1.2 fusion.30
  9.2 1.2 fusion.32
  10.5 103.7 %all-gather.4.cloned.1.call-done = bf16[512,1536]{1,0:T(8,128)(2,1)} async-done(((bf16[32,1536]{1,0:T(8,128)(2,1)}), bf16[512,1536]{1,0:T(8,128)(2,1)}) %all-gather.4.cloned.1.call-update) | async-done | bytes 1572880 | tf_op jit(solution)/shard_map/all_gather | solution.py:38
  114.2 2.4 convolution_convert_fusion
  116.6 1.1 copy-done.2
  118.6 3.2 collective-permute-start
  121.7 6.3 %collective-permute-start.1 = (bf16[4,128,1024]{1,2,0:T(8,128)(2,1)S(1)}, bf16[4,128,1024]{1,2,0:T(8,128)(2,1)}, u32[]{:S(2)}, u32[]{:S(2)}) collective-permute-start(bf16[4,128,1024]{1,2,0:T(8,128)(2,1)S(1)} %copy.80), channel_id=1, source_target_pairs={{0,16},{16,32},{32,48},{48,64},{64,80},{80,96},{96,112},{112,128},... | collective-permute-start | bytes 3145736 | tf_op jit(solution)/shard_map/ppermute | solution.py:12
  128.2 115.8 %all_gather.13 = bf16[512,512]{1,0:T(8,128)(2,1)} all-gather(bf16[32,512]{1,0:T(8,128)(2,1)S(1)} %copy-done.4), channel_id=1, replica_groups=mesh['tm'=32,'zone'=16] {'zone'}, dimensions={0}, use_global_device_ids=true | all-gather | bytes 557056 | tf_op jit(solution)/shard_map/all_gather | solution.py:39
  244.0 1.1 slice.20
  245.4 1.2 copy.61
  246.6 1.4 pad_maximum_fusion
  248.2 3.0 copy.62
  251.3 2.9 copy.63
  254.2 3.0 fusion.46
  257.2 2.5 fusion.26
  261.0 1.1 copy.66
  262.0 3.5 all-to-all-start
  266.6 26.0 %all-to-all-done = bf16[4,512,128]{2,0,1:T(4,128)(2,1)S(1)} async-done(((bf16[4,512,128]{2,0,1:T(4,128)(2,1)}), bf16[4,512,128]{2,0,1:T(4,128)(2,1)S(1)}, u32[]{:S(2)}, u32[]{:S(2)}) %all-to-all-start) | async-done | bytes 524320 | tf_op jit(solution)/shard_map/all_to_all | solution.py:96
  292.7 0.8 gather_fusion
  293.5 3.1 fusion.27
  296.6 2.8 copy.78
  299.3 2.7 reshape.152
  302.0 39.8 %all_to_all.24 = bf16[16,2,8192]{2,1,0:T(2,128)(2,1)} all-to-all(bf16[16,2,8192]{2,1,0:T(2,128)(2,1)} %reshape.152), channel_id=1, replica_groups=mesh['tm'=32,'zone'=16] {'zone'}, dimensions={0} | all-to-all | bytes 1048576 | tf_op jit(solution)/shard_map/all_to_all | solution.py:103
  341.8 3.6 reshape.153
  345.4 2.2 copy.72
  347.6 1.2 copy.82
  349.9 1.0 multiply_convert_fusion
  350.9 18.6 %all-gather.8.cloned.1.call-done = bf16[2048,512]{1,0:T(8,128)(2,1)} async-done(((bf16[128,512]{1,0:T(8,128)(2,1)}), bf16[2048,512]{1,0:T(8,128)(2,1)}) %all-gather.8.cloned.1.call-update) | async-done | bytes 2097168 | tf_op jit(solution)/shard_map/all_gather | solution.py:41
  369.5 5.0 %fusion.9 = f32[512,512]{1,0:T(8,128)S(1)} fusion(bf16[2048,512]{1,0:T(8,128)(2,1)} %all-gather.8.cloned.1.call-done, bf16[512,512]{1,0:T(8,128)(2,1)} %bitcast.99, bf16[512,2048]{1,0:T(8,128)(2,1)} %all-gather.6.cloned.1.call-done), kind=kOutput, calls=%fused_computation.13 | convolution fusion | flops 2156920832 | bytes 5767168 | tf_op jit(solution)/shard_map/dot_general | solution.py:109
  374.5 1.1 add_convert_fusion
  (52 shorter events, 4.8 us)
Async XLA Ops:
  6.5 107.7 %all-gather.4.cloned.1.call-start = ((), (), s32[]{:S(2)}) async-start(), calls=%async_computation.2 | async-start | bytes 1671168 | tf_op jit(solution)/shard_map/all_gather | solution.py:38
  7.3 343.6 %all-gather.6.cloned.1.call-start = ((), (), s32[]{:S(2)}) async-start(), calls=%async_computation.3 | async-start | bytes 2228224 | tf_op jit(solution)/shard_map/all_gather | solution.py:40
  116.6 1.2 copy-start.2
  117.8 10.3 %copy-start.9 = (s32[1,2]{1,0:T(1,128)S(1)}, s32[1,2]{1,0:T(1,128)}, u32[]{:S(2)}) copy-start(s32[1,2]{1,0:T(1,128)} %param.16) | copy-start | bytes 28
  117.8 10.4 %copy-start.4 = (bf16[32,512]{1,0:T(8,128)(2,1)S(1)}, bf16[32,512]{1,0:T(8,128)(2,1)}, u32[]{:S(2)}) copy-start(bf16[32,512]{1,0:T(8,128)(2,1)} %param.15) | copy-start | bytes 98308
  118.6 128.0 %collective-permute-start = (bf16[4,128,1024]{1,2,0:T(8,128)(2,1)S(1)}, bf16[4,128,1024]{1,2,0:T(8,128)(2,1)S(1)}, u32[]{:S(2)}, u32[]{:S(2)}) collective-permute-start(bf16[4,128,1024]{1,2,0:T(8,128)(2,1)S(1)} %copy.80), channel_id=1, source_target_pairs={{0,32},{16,48},{32,64},{48,80},{64,96},{80,112},{96,128},{112,144}... | collective-permute-start | bytes 3145736 | tf_op jit(solution)/shard_map/ppermute | solution.py:12
  121.7 124.9 %collective-permute-start.1 = (bf16[4,128,1024]{1,2,0:T(8,128)(2,1)S(1)}, bf16[4,128,1024]{1,2,0:T(8,128)(2,1)}, u32[]{:S(2)}, u32[]{:S(2)}) collective-permute-start(bf16[4,128,1024]{1,2,0:T(8,128)(2,1)S(1)} %copy.80), channel_id=1, source_target_pairs={{0,16},{16,32},{32,48},{48,64},{64,80},{80,96},{96,112},{112,128},... | collective-permute-start | bytes 3145736 | tf_op jit(solution)/shard_map/ppermute | solution.py:12
  251.3 2.9 copy-start.3
  257.2 3.0 copy-start
  257.2 3.0 copy-start.1
  259.7 1.1 copy-start.5
  260.8 5.5 %copy-start.7 = (s32[16,3]{0,1:T(4,128)S(1)}, s32[16,3]{0,1:T(4,128)}, u32[]{:S(2)}) copy-start(s32[16,3]{0,1:T(4,128)} %param.18) | copy-start | bytes 580
  260.8 5.7 %copy-start.8 = (s32[16]{0:T(128)S(1)}, s32[16]{0:T(128)}, u32[]{:S(2)}) copy-start(s32[16]{0:T(128)} %param.19) | copy-start | bytes 196
  262.0 30.5 %all-to-all-start = ((bf16[4,512,128]{2,0,1:T(4,128)(2,1)}), bf16[4,512,128]{2,0,1:T(4,128)(2,1)S(1)}, u32[]{:S(2)}, u32[]{:S(2)}) async-start(bf16[4,512,128]{2,0,1:T(4,128)(2,1)} %copy.66), calls=%async_computation | async-start | bytes 1048576 | tf_op jit(solution)/shard_map/all_to_all | solution.py:96
  265.6 103.9 %all-gather.8.cloned.1.call-start = ((), (), s32[]{:S(2)}) async-start(), calls=%async_computation.4 | async-start | bytes 2228224 | tf_op jit(solution)/shard_map/all_gather | solution.py:41
  349.2 0.7 copy-start.6
Sparse Core Ops, SparseCore 0:
  9.4 104.7 all-gather.3
  116.3 143.4 all-gather.5
  268.5 100.9 all-gather.7
where the time goes:
time: 383 us; the launch traced here: 382 us
  blocking collectives  156 us (41%)
  waiting for transfers between devices  150 us (39%)
  local copies, waits for them, and re-layouts  26.5 us (7%)
  matrix products  16.5 us (4%)
  between operations  13.4 us (3%)
  starting transfers between devices  13 us (3%)
  other arithmetic  6.54 us (2%)
    all_gather x1, blocking collectives, on_device(): lax.all_gather(w_out_attn, 'zone', axis=0, tiled=True)  116 us
    all_gather x1, waiting for transfers between devices, on_device(): lax.all_gather(w_qkv, 'zone', axis=0, tiled=True)  104 us
    all_to_all x1, blocking collectives, on_device(): lax.all_to_all(spatial, 'zone', split_axis=2, concat_axis=1, tiled=True)  39.8 us
    all_to_all x1, waiting for transfers between devices, on_device(): lax.all_to_all(mixin, 'zone', split_axis=1, concat_axis=2, tiled=True)  26 us
    all_gather x1, waiting for transfers between devices, on_device(): lax.all_gather(w_out, 'zone', axis=0, tiled=True)  18.6 us
    unnamed x25, local copies, waits for them, and re-layouts  9.7 us
    ppermute x2, starting transfers between devices, shifted(): lax.ppermute(value, axis, [(source, source + steps) for source in range(f...  9.44 us
  transfers between devices with their start and end apart: 6, of which 3 were waited for; matrix products, arithmetic and copies ran while one was open for 11% of the time, Pallas kernels for 0%

commit v1 on v0

v1 whole, which is shorter than its diff:
```python
import functools

import jax
import jax.numpy as jnp
from jax import lax
from jax.experimental import pallas as pl
from jax.experimental.pallas import tpu as pltpu
from jax.sharding import PartitionSpec as P

MESH = pl.DeviceIdType.MESH
HEADS = 4
HD = 128
NG = 4
ZC = 32
F32, BF16 = jnp.float32, jnp.bfloat16

SLOTS = [(d, f, 0) for d in (3, -3, 2, -2, 1, -1, 0) for f in (0, 1) if (d, f) != (0, 0)]
SLOTS += [(d, f, 1) for d in (4, -4) for f in (0, 1)]
RING = (-3, 3, 4, -2, 2, -1, 1)
XY = [(dx, dy) for dx in range(4) for dy in range(4) if dx or dy]


def rms(values, gain):
    mean_sq = jnp.mean(values * values, axis=-1, keepdims=True)
    return values * lax.rsqrt(mean_sq + 1e-06) * gain


def dot(a, b):
    return jnp.dot(a, b, preferred_element_type=F32)


def kernel(
    states, w_qkv, w_attn, w_in, w_out, mix, pat, g_attn, g_mix, g_ffn, neighbours, degree,
    out,
    st, wq, wa, wi, wo, mx, pats, nrm, kv, qs, ctx, aa, after, mixin, xm, stage, spat, nf, acc,
    loc_sem, ag1_s, ag1_r, ag2_s, ag2_r, ag3_s, ag3_r, e1_s, e1_r, ep_s, ep_r, e2_s, e2_r,
    fw_s, fw_r, rt_s, rt_r,
):
    tm, zone = lax.axis_index("tm"), lax.axis_index("zone")
    h, col = lax.rem(tm, 2), tm // 2
    x, y = lax.rem(col, 4), col // 4
    zl, c = zone // 2, lax.rem(zone, 2)
    z = h * 8 + zl
    p = col

    def at_z(d, flip):
        zz = lax.rem(z + d + 16, 16)
        return (col * 2 + zz // 8, lax.rem(zz, 8) * 2 + lax.rem(c + flip, 2))

    def at_xy(dx, dy):
        xx, yy = lax.rem(x + dx, 4), lax.rem(y + dy, 4)
        return ((yy * 4 + xx) * 2 + h, zone)

    following = (lax.rem(col + 1, 16) * 2 + h, zone)
    partner = at_z(8, 0)
    other = at_z(0, 1)

    def remote(src, dst, ssem, rsem, dev):
        return pltpu.make_async_remote_copy(
            src, dst, ssem, rsem, device_id=dev, device_id_type=MESH
        )

    locals_ = [
        pltpu.make_async_copy(states, st.at[2 + h], loc_sem.at[0]),
        pltpu.make_async_copy(mix, mx, loc_sem.at[1]),
    ]
    r8, c8 = p // 8, pl.multiple_of(lax.rem(p, 8) * 128, 128)
    p8 = lax.rem(p, 8)
    r4, c4 = p8 // 4, pl.multiple_of(lax.rem(p8, 4) * 128, 128)
    i8 = pl.multiple_of(lax.rem(p, 8) * 256, 256)
    g2, h2 = p // 2, pl.multiple_of(lax.rem(p, 2) * 256, 256)
    first = p < 8

    src_kv = w_qkv.at[pl.ds(pl.multiple_of(r8 * 16, 16), 16), pl.ds(512 + c8, 128)]
    src_q = w_qkv.at[pl.ds(pl.multiple_of(r4 * 16, 16), 16), pl.ds(c4, 128)]
    src_a = w_attn.at[pl.ds(pl.multiple_of(r4 * 16, 16), 16), pl.ds(c4, 128)]
    src_i = w_in.at[pl.ds(pl.multiple_of(r8 * 16, 16), 16), pl.ds(i8, 256)]
    src_o = w_out.at[pl.ds(pl.multiple_of(g2 * 16, 16), 16), pl.ds(h2, 256)]

    def own_kv(zz):
        return wq.at[zz, c, r8, :, pl.ds(512 + c8, 128)]

    def own_q(zz):
        return wq.at[zz, c, r4, :, pl.ds(c4, 128)]

    def own_a(zz):
        return wa.at[zz, c, r4, :, pl.ds(c4, 128)]

    def own_i(zz):
        return wi.at[zz, c, r8, :, pl.ds(i8, 256)]

    def own_o(zz):
        return wo.at[zz, c, g2, :, pl.ds(h2, 256)]

    pieces = ((src_kv, own_kv), (src_i, own_i), (src_o, own_o))
    every = pl.ds(0, 8)

    for cp in locals_:
        cp.start()
    for n, (src, own) in enumerate(pieces):
        pltpu.make_async_copy(src, own(zl), loc_sem.at[2 + n]).start()

    @pl.when(first)
    def _():
        pltpu.make_async_copy(src_q, own_q(zl), loc_sem.at[5]).start()

    @pl.when(jnp.logical_not(first))
    def _():
        pltpu.make_async_copy(src_a, own_a(zl), loc_sem.at[5]).start()

    barrier = pltpu.get_barrier_semaphore()
    for d in range(16):
        for f in (0, 1):
            if (d, f) != (0, 0):
                pl.semaphore_signal(barrier, inc=1, device_id=at_z(d, f), device_id_type=MESH)
    for dx, dy in XY:
        pl.semaphore_signal(barrier, inc=1, device_id=at_xy(dx, dy), device_id_type=MESH)
    pl.semaphore_wait(barrier, 46)

    def chunk(ref, g):
        return ref.at[:, pl.ds(pl.multiple_of(g * ZC, ZC), ZC), :]

    def swap(g):
        return remote(chunk(states, g), chunk(st.at[2 + h], g), e1_s.at[g], e1_r.at[g], partner)

    def swapped(g):
        return remote(chunk(states, g), chunk(st.at[3 - h], g), e1_s.at[g], e1_r.at[g], partner)

    def onward(g):
        return remote(
            chunk(states, g), chunk(st.at[h], g), e2_s.at[0, g], e2_r.at[0, g], following
        )

    def relay(g):
        return remote(
            chunk(st.at[3 - h], g), chunk(st.at[1 - h], g), e2_s.at[1, g], e2_r.at[1, g], following
        )

    def ag1(n, src, own, k):
        return remote(src, own(zl), ag1_s.at[n, k], ag1_r.at[n, k], at_z(RING[k], 0))

    send_pat = remote(pat, pats.at[h], ep_s, ep_r, partner)
    send_pat.start()
    swap(0).start()
    for k in range(7):
        ag1(0, src_kv, own_kv, k).start()

    @pl.when(first)
    def _():
        for k in range(7):
            ag1(3, src_q, own_q, k).start()

    @pl.when(jnp.logical_not(first))
    def _():
        for k in range(7):
            ag1(3, src_a, own_a, k).start()

    for g in range(NG):
        if g:
            swap(g).start()
        onward(g).start()
    for k in range(7):
        ag1(1, src_i, own_i, k).start()
        ag1(2, src_o, own_o, k).start()
    pats[pl.ds(h, 1)] = pat[...].reshape(1, 8, 128)

    def ag2(n, own, k):
        return remote(own(every), own(every), ag2_s.at[n, k], ag2_r.at[n, k], at_xy(*XY[k]))

    for n in (0, 3):
        src, own = pieces[0] if n == 0 else (src_q, own_q)
        pltpu.make_async_copy(src, own(zl), loc_sem.at[2 if n == 0 else 5]).wait()
        for k in range(7):
            ag1(n, src, own, k).wait_recv()
    for k in range(15):
        ag2(0, own_kv, k).start()

    @pl.when(first)
    def _():
        for k in range(15):
            ag2(3, own_q, k).start()

    @pl.when(jnp.logical_not(first))
    def _():
        for k in range(15):
            ag2(3, own_a, k).start()

    for k in range(15):
        ag2(0, own_kv, k).wait_recv()
        ag2(3, own_q, k).wait_recv()

    def ag3(n, w):
        return remote(w.at[:, c], w.at[:, c], ag3_s.at[n], ag3_r.at[n], other)

    ag3(0, wq).start()
    ag3(1, wa).start()
    for n in (1, 2):
        src, own = pieces[n]
        pltpu.make_async_copy(src, own(zl), loc_sem.at[2 + n]).wait()
        for k in range(7):
            ag1(n, src, own, k).wait_recv()
    locals_[0].wait()
    send_pat.wait_recv()
    ag3(0, wq).wait_recv()
    ag3(1, wa).wait_recv()
    wq2, wa2 = wq.reshape(512, 1536), wa.reshape(512, 512)

    rows = lax.broadcasted_iota(jnp.int32, (128, 128), 0)
    cols = lax.broadcasted_iota(jnp.int32, (128, 128), 1)
    same = lax.rem(rows, ZC) == lax.rem(cols, ZC)
    causal = same & (cols // ZC <= rows // ZC)

    def fw(slot, g):
        d, f, half = SLOTS[slot]
        zz = lax.rem(z + d + 16, 16)
        m = lax.rem(zz, 8) * 2 + lax.rem(c + f, 2)
        low = g * ZC + (ZC // 2 if d == -4 else 0)
        span = pl.ds(pl.multiple_of(low, 16), ZC // 2 if half else ZC)
        return remote(
            mixin.at[zz // 8, m // 4, lax.rem(m, 4), span],
            xm.at[zone, span],
            fw_s.at[slot],
            fw_r.at[slot],
            at_z(d, f),
        )

    def step(g, carry):
        z0 = pl.multiple_of(g * ZC, ZC)
        swapped(g).wait_recv()
        relay(g).start()
        onward(g).wait_recv()
        relay(g).wait_recv()
        for b in range(4):
            block = st[b, :, pl.ds(z0, ZC), :].reshape(128, 512).astype(F32)
            nrm[b * 128 : (b + 1) * 128, :] = rms(block, g_attn[...]).astype(BF16)
        for j in range(2):
            kv[:, j * 512 : (j + 1) * 512] = dot(
                nrm[...], wq2[:, (j + 1) * 512 : (j + 2) * 512]
            ).astype(BF16)
        qs[...] = dot(nrm[256:512, :], wq2[:, 0:512]).astype(BF16)
        for t in range(2):
            gone = (col * 2 + t) >= 1
            ok1 = jnp.where(gone, pats[t, 0:1, :], 0.0)
            ok2 = jnp.where((col * 2 + t) >= 2, pats[t, 4:5, :], 0.0)
            allowed = jnp.concatenate(
                [same & (ok2 > 0.5), same & (ok1 > 0.5), causal], axis=1
            )
            for hd in range(HEADS):
                q = qs[t * 128 : (t + 1) * 128, hd * HD : (hd + 1) * HD]
                k = kv[t * 128 : t * 128 + 384, hd * HD : (hd + 1) * HD]
                v = kv[t * 128 : t * 128 + 384, 512 + hd * HD : 512 + (hd + 1) * HD]
                s = lax.dot_general(q, k, (((1,), (1,)), ((), ())), preferred_element_type=F32)
                s = jnp.where(allowed, s * HD**-0.5, -1e30)
                e = jnp.exp(s - jnp.max(s, axis=-1, keepdims=True))
                total = jnp.sum(e, axis=-1, keepdims=True)
                got = dot(e.astype(BF16), v) / total
                ctx[t * 128 : (t + 1) * 128, hd * HD : (hd + 1) * HD] = got.astype(BF16)
        for t in range(2):
            block = st[2 + t, :, pl.ds(z0, ZC), :].reshape(128, 512).astype(F32)
            wide = block + dot(ctx[t * 128 : (t + 1) * 128, :], wa2[...])
            aa[t] = wide
            mi = rms(wide, g_mix[...]).astype(BF16)
            for j in range(4):
                mixin[t, :, j, pl.ds(z0, ZC), :] = mi[:, j * 128 : (j + 1) * 128].reshape(
                    4, ZC, 128
                )
        for slot in range(len(SLOTS)):
            fw(slot, g).start()
        after[:, pl.ds(z0, ZC), :] = aa[h].reshape(4, ZC, 512)
        xm[zone, pl.ds(z0, ZC), :] = mixin[h, zone // 4, lax.rem(zone, 4), pl.ds(z0, ZC), :]
        return carry

    lax.fori_loop(0, NG, step, 0)

    for k in range(15):
        ag2(1, own_i, k).start()
        ag2(2, own_o, k).start()

    locals_[1].wait()
    for slot, (d, f, half) in enumerate(SLOTS):
        span = pl.ds(0, 64 if half else 128)
        remote(
            mixin.at[0, 0, 0, span], xm.at[zone, span], fw_s.at[slot], fw_r.at[slot], other
        ).wait()

    def mixed(b):
        total = jnp.zeros((128, 128), F32)
        for k in range(3):
            weight = mx[b, k]
            live = jnp.where(k < degree[b], weight, jnp.zeros_like(weight))
            total += dot(live, xm[neighbours[b, k]])
        return total.astype(BF16)

    def back(o):
        b = lax.rem(zone + o, 16)
        return remote(stage.at[b], spat.at[zone], rt_s.at[o], rt_r.at[o], (tm, b))

    def send_back(o, carry):
        b = lax.rem(zone + o, 16)
        stage[b] = mixed(b)
        back(o).start()
        return carry

    lax.fori_loop(1, 16, send_back, 0)
    spat[zone] = mixed(zone)

    for k in range(15):
        ag2(1, own_i, k).wait_recv()
        ag2(2, own_o, k).wait_recv()
    ag3(2, wi).start()
    ag3(3, wo).start()

    send_pat.wait_send()
    for g in range(NG):
        swap(g).wait_send()
        onward(g).wait_send()
        relay(g).wait_send()
    for k in range(7):
        ag1(0, src_kv, own_kv, k).wait_send()
        ag1(1, src_i, own_i, k).wait_send()
        ag1(2, src_o, own_o, k).wait_send()
        ag1(3, src_q, own_q, k).wait_send()
    for k in range(15):
        ag2(0, own_kv, k).wait_send()
        ag2(1, own_i, k).wait_send()
        ag2(2, own_o, k).wait_send()
        ag2(3, own_q, k).wait_send()
    ag3(0, wq).wait_send()
    ag3(1, wa).wait_send()
    ag3(2, wi).wait()
    ag3(3, wo).wait()

    wi2, wo2 = wi.reshape(512, 2048), wo.reshape(2048, 512)
    for o in range(1, 16):
        back(o).wait()
    for half in range(2):
        for i in range(2):
            t = half * 2 + i
            wide = after[t] + jnp.concatenate(
                [spat[t * 4 + j].astype(F32) for j in range(4)], axis=1
            )
            acc[i * 128 : (i + 1) * 128, :] = wide
            nf[i * 128 : (i + 1) * 128, :] = rms(wide, g_ffn[...]).astype(BF16)
        for j in range(4):
            hidden = jax.nn.gelu(
                dot(nf[...], wi2[:, j * 512 : (j + 1) * 512]), approximate=True
            ).astype(BF16)
            acc[...] += dot(hidden, wo2[j * 512 : (j + 1) * 512, :])
        out[half * 2 : half * 2 + 2] = acc[...].astype(BF16).reshape(2, 128, 512)


def on_device(
    states, gain_attn, w_qkv, w_out_attn, pattern, gain_mix, neighbours, degree, mix, gain_ffn,
    w_in, w_out,
):
    pat = jnp.broadcast_to(
        jnp.repeat(pattern.reshape(2, 1).astype(F32), 4, axis=0), (8, 128)
    )
    hbm = pl.BlockSpec(memory_space=pl.ANY)
    vmem = pl.BlockSpec(memory_space=pltpu.VMEM)
    smem = pl.BlockSpec(memory_space=pltpu.SMEM)
    dma = pltpu.SemaphoreType.DMA
    return pl.pallas_call(
        kernel,
        out_shape=jax.ShapeDtypeStruct(states.shape, BF16),
        in_specs=[hbm] * 6 + [vmem] * 4 + [smem] * 2,
        out_specs=vmem,
        scratch_shapes=[
            pltpu.VMEM((4, 4, 128, 512), BF16),
            pltpu.VMEM((8, 2, 2, 16, 1536), BF16),
            pltpu.VMEM((8, 2, 2, 16, 512), BF16),
            pltpu.VMEM((8, 2, 2, 16, 2048), BF16),
            pltpu.VMEM((8, 2, 8, 16, 512), BF16),
            pltpu.VMEM((16, 3, 128, 128), BF16),
            pltpu.VMEM((2, 8, 128), F32),
            pltpu.VMEM((512, 512), BF16),
            pltpu.VMEM((512, 1024), BF16),
            pltpu.VMEM((256, 512), BF16),
            pltpu.VMEM((256, 512), BF16),
            pltpu.VMEM((2, 128, 512), F32),
            pltpu.VMEM((4, 128, 512), F32),
            pltpu.VMEM((2, 4, 4, 128, 128), BF16),
            pltpu.VMEM((16, 128, 128), BF16),
            pltpu.VMEM((16, 128, 128), BF16),
            pltpu.VMEM((16, 128, 128), BF16),
            pltpu.VMEM((256, 512), BF16),
            pltpu.VMEM((256, 512), F32),
            dma((6,)),
            dma((4, 7)), dma((4, 7)),
            dma((4, 15)), dma((4, 15)),
            dma((4,)), dma((4,)),
            dma((NG,)), dma((NG,)),
            dma, dma,
            dma((2, NG)), dma((2, NG)),
            dma((len(SLOTS),)), dma((len(SLOTS),)),
            dma((16,)), dma((16,)),
        ],
        compiler_params=pltpu.CompilerParams(
            collective_id=0, has_side_effects=True, vmem_limit_bytes=48 << 20
        ),
        cost_estimate=pl.CostEstimate(
            flops=5 * 10**9, bytes_accessed=8 * 10**6, transcendentals=2 * 10**6
        ),
        name="layer",
    )(
        states, w_qkv, w_out_attn, w_in, w_out, mix, pat,
        gain_attn.reshape(1, -1), gain_mix.reshape(1, -1), gain_ffn.reshape(1, -1),
        neighbours, degree,
    )


def solution(mesh):
    return jax.shard_map(
        on_device,
        mesh=mesh,
        in_specs=(
            P("tm", "zone", None),
            P(),
            P("zone", None),
            P("zone", None),
            P("tm", None),
            P(),
            P(),
            P(),
            P(),
            P(),
            P("zone", None),
            P("zone", None),
        ),
        out_specs=P("tm", "zone", None),
        check_vma=False,
    )
```

time: 383 us -> 150 us (0.39)
  blocking collectives: 156 us -> 0 us
  waiting for transfers between devices: 150 us -> 0 us
  Pallas kernels: 0 us -> 138 us
  matrix products: 16.5 us -> 0 us
  local copies, waits for them, and re-layouts: 26.5 us -> 10.4 us
  between operations: 13.4 us -> 0.02 us
  starting transfers between devices: 13 us -> 0 us
  other arithmetic: 6.54 us -> 0.66 us
    pallas_call x0 -> x1, Pallas kernels: none -> 138 us  [on_device(): pl.pallas_call(kernel, out_shape=jax.ShapeDtypeStruct(states.shape, BF16)...]
    all_gather x3 -> x0, waiting for transfers between devices: 122 us -> none  [the longest x1 104 us: on_device(): lax.all_gather(w_qkv, 'zone', axis=0, tiled=True)]
    all_gather x1 -> x0, blocking collectives: 116 us -> none  [on_device(): lax.all_gather(w_out_attn, 'zone', axis=0, tiled=True)]
    all_to_all x1 -> x0, blocking collectives: 39.8 us -> none  [on_device(): lax.all_to_all(spatial, 'zone', split_axis=2, concat_axis=1, tiled=True)]
    all_to_all x1 -> x0, waiting for transfers between devices: 26 us -> none  [on_device(): lax.all_to_all(mixin, 'zone', split_axis=1, concat_axis=2, tiled=True)]
    dot_general x5 -> x0, matrix products: 13.5 us -> none  [the longest x1 4.98 us: on_device(): jnp.dot(hidden, full_out, preferred_element_type=jnp.float32)]
    reshape x4 -> x0, local copies, waits for them, and re-layouts: 9.88 us -> none  [the longest x1 3.02 us: on_device(): all_pairs[..., :width].reshape(key_count, zone_rows, HEADS, head_size)]
    ppermute x2 -> x0, starting transfers between devices: 9.44 us -> none  [shifted(): lax.ppermute(value, axis, [(source, source + steps) for source in range(f...]
  transfers between devices with their start and end apart: 6 -> 0, of which waited for: 3 -> 0; matrix products, arithmetic and copies ran while one was open for 11% -> 0% of each run, Pallas kernels for 0% -> 0%
where the time goes in v1:
time: 150 us; the launch traced here: 149 us
  Pallas kernels  138 us (92%)
  local copies, waits for them, and re-layouts  10.4 us (7%)
    pallas_call x1, Pallas kernels, on_device(): pl.pallas_call(kernel, out_shape=jax.ShapeDtypeStruct(states.shape, BF16)...  138 us
    unnamed x22, local copies, waits for them, and re-layouts  10.2 us

profile of v1, /device:TPU:1, one launch (start us, length us, event | category | flops | bytes accessed | tf_op | source)
XLA Modules:
  0.0 149.2 jit_solution(2465246391469832773)
XLA Ops:
  0.0 0.7 convert_bitcast_fusion
  0.7 0.1 broadcast_in_dim.10
  0.7 0.1 broadcast_in_dim.11
  0.8 0.1 broadcast_in_dim.12.pat
  0.9 0.8 copy.13.neighbours
  1.6 0.0 copy-start
  1.6 1.4 copy-done
  3.1 0.0 copy-start.1
  3.1 1.0 copy-done.1
  4.1 0.0 copy-start.2
  4.1 0.9 copy-done.2
  5.0 0.0 copy-start.3
  5.0 0.9 copy-done.3
  5.9 0.0 copy-start.4
  5.9 0.9 copy-done.4
  6.8 0.0 copy-start.5
  6.8 0.8 copy-done.5
  7.6 0.0 copy-start.6
  7.6 0.7 copy-done.6
  8.2 0.0 copy-start.7
  8.2 0.7 copy-done.7
  8.9 0.0 copy-start.8
  8.9 0.7 copy-done.8
  9.6 0.0 copy-start.9
  9.6 0.7 copy-done.9
  10.3 138.2 %layer.1 = bf16[4,128,512]{2,1,0:T(8,128)(2,1)S(1)} custom-call(bf16[4,128,512]{2,1,0:T(8,128)(2,1)S(1)} %copy-done.1, bf16[32,1536]{1,0:T(8,128)(2,1)S(1)} %copy-done.4, bf16[32,512]{1,0:T(8,128)(2,1)S(1)} %copy-done.5, bf16[32,2048]{1,0:T(8,128)(2,1)S(1)} %copy-done.2, bf16[128,512]{1,0:T(8,128)(2,1)S(1)} %copy-done.3, ...), custom_call_target="tpu_custom_call" | custom-call | flops 5000000000 | bytes 8000000 | tf_op jit(solution)/shard_map/layer/pallas_call | solution.py:363
  148.4 0.8 copy.15
Async XLA Ops:
  1.6 1.4 copy-start
  3.1 1.0 copy-start.1
  4.1 0.9 copy-start.2
  5.0 0.9 copy-start.3
  5.9 0.9 copy-start.4
  6.8 0.8 copy-start.5
  7.6 0.7 copy-start.6
  8.2 0.7 copy-start.7
  8.9 0.7 copy-start.8
  9.6 0.7 copy-start.9

commit v2 on v1

--- a/solution.py
+++ b/solution.py
@@ -10,12 +10,12 @@
 MESH = pl.DeviceIdType.MESH
 HEADS = 4
 HD = 128
-NG = 4
-ZC = 32
+NG = 8
+ZC = 16
+R = 4 * ZC
 F32, BF16 = jnp.float32, jnp.bfloat16
 
-SLOTS = [(d, f, 0) for d in (3, -3, 2, -2, 1, -1, 0) for f in (0, 1) if (d, f) != (0, 0)]
-SLOTS += [(d, f, 1) for d in (4, -4) for f in (0, 1)]
+SLOTS = [(d, f) for d in (4, 3, -3, 2, -2, 1, -1, 0) for f in (0, 1) if (d, f) != (0, 0)]
 RING = (-3, 3, 4, -2, 2, -1, 1)
 XY = [(dx, dy) for dx in range(4) for dy in range(4) if dx or dy]
 
@@ -30,9 +30,9 @@
 
 
 def kernel(
-    states, w_qkv, w_attn, w_in, w_out, mix, pat, g_attn, g_mix, g_ffn, neighbours, degree,
+    states, w_qkv, w_attn, w_in, w_out, mix, gains_a, gains_m, gains_f, pat_in, near_in, degree_in,
     out,
-    st, wq, wa, wi, wo, mx, pats, nrm, kv, qs, ctx, aa, after, mixin, xm, stage, spat, nf, acc,
+    pat, g_attn, g_mix, g_ffn, pattern, neighbours, degree, st, wq, wa, wi, wo, mx, pats, nrm, kv, qs, ctx, aa, after, mixin, xm, stage, spat, nf, acc,
     loc_sem, ag1_s, ag1_r, ag2_s, ag2_r, ag3_s, ag3_r, e1_s, e1_r, ep_s, ep_r, e2_s, e2_r,
     fw_s, fw_r, rt_s, rt_r,
 ):
@@ -63,6 +63,12 @@
     locals_ = [
         pltpu.make_async_copy(states, st.at[2 + h], loc_sem.at[0]),
         pltpu.make_async_copy(mix, mx, loc_sem.at[1]),
+        pltpu.make_async_copy(pat_in, pattern, loc_sem.at[6]),
+        pltpu.make_async_copy(gains_a, g_attn, loc_sem.at[7]),
+        pltpu.make_async_copy(gains_m, g_mix, loc_sem.at[8]),
+        pltpu.make_async_copy(gains_f, g_ffn, loc_sem.at[9]),
+        pltpu.make_async_copy(near_in, neighbours, loc_sem.at[10]),
+        pltpu.make_async_copy(degree_in, degree, loc_sem.at[11]),
     ]
     r8, c8 = p // 8, pl.multiple_of(lax.rem(p, 8) * 128, 128)
     p8 = lax.rem(p, 8)
@@ -115,6 +121,10 @@
                 pl.semaphore_signal(barrier, inc=1, device_id=at_z(d, f), device_id_type=MESH)
     for dx, dy in XY:
         pl.semaphore_signal(barrier, inc=1, device_id=at_xy(dx, dy), device_id_type=MESH)
+    locals_[2].wait()
+    upper = lax.broadcasted_iota(jnp.int32, (8, 256), 0) < 4
+    pat[...] = jnp.where(upper, pattern[0, 0], pattern[0, 1]).astype(F32)
+    pats[pl.ds(h, 1)] = pat[...].reshape(1, 8, 256)
     pl.semaphore_wait(barrier, 46)
 
     def chunk(ref, g):
@@ -140,8 +150,6 @@
         return remote(src, own(zl), ag1_s.at[n, k], ag1_r.at[n, k], at_z(RING[k], 0))
 
     send_pat = remote(pat, pats.at[h], ep_s, ep_r, partner)
-    send_pat.start()
-    swap(0).start()
     for k in range(7):
         ag1(0, src_kv, own_kv, k).start()
 
@@ -155,14 +163,11 @@
         for k in range(7):
             ag1(3, src_a, own_a, k).start()
 
+    send_pat.start()
     for g in range(NG):
-        if g:
-            swap(g).start()
-        onward(g).start()
-    for k in range(7):
-        ag1(1, src_i, own_i, k).start()
-        ag1(2, src_o, own_o, k).start()
-    pats[pl.ds(h, 1)] = pat[...].reshape(1, 8, 128)
+        swap(g).start()
+        if g < 2:
+            onward(g).start()
 
     def ag2(n, own, k):
         return remote(own(every), own(every), ag2_s.at[n, k], ag2_r.at[n, k], at_xy(*XY[k]))
@@ -185,6 +190,11 @@
         for k in range(15):
             ag2(3, own_a, k).start()
 
+    for g in range(2, NG):
+        onward(g).start()
+    for k in range(7):
+        ag1(1, src_i, own_i, k).start()
+        ag1(2, src_o, own_o, k).start()
     for k in range(15):
         ag2(0, own_kv, k).wait_recv()
         ag2(3, own_q, k).wait_recv()
@@ -194,28 +204,28 @@
 
     ag3(0, wq).start()
     ag3(1, wa).start()
-    for n in (1, 2):
-        src, own = pieces[n]
-        pltpu.make_async_copy(src, own(zl), loc_sem.at[2 + n]).wait()
-        for k in range(7):
-            ag1(n, src, own, k).wait_recv()
     locals_[0].wait()
+    for n in (3, 4, 5, 6, 7):
+        locals_[n].wait()
     send_pat.wait_recv()
     ag3(0, wq).wait_recv()
     ag3(1, wa).wait_recv()
     wq2, wa2 = wq.reshape(512, 1536), wa.reshape(512, 512)
 
-    rows = lax.broadcasted_iota(jnp.int32, (128, 128), 0)
-    cols = lax.broadcasted_iota(jnp.int32, (128, 128), 1)
+    rows = lax.broadcasted_iota(jnp.int32, (R, 3 * R), 0)
+    cols = lax.broadcasted_iota(jnp.int32, (R, 3 * R), 1)
     same = lax.rem(rows, ZC) == lax.rem(cols, ZC)
-    causal = same & (cols // ZC <= rows // ZC)
+    segment = cols // R
+    causal = same & (segment == 2) & (lax.rem(cols, R) // ZC <= rows // ZC)
+    back1, back2 = same & (segment == 1), same & (segment == 0)
 
     def fw(slot, g):
-        d, f, half = SLOTS[slot]
+        d, f = SLOTS[slot]
+        if d == 4:
+            d = 4 - 8 * lax.rem(g, 2)
         zz = lax.rem(z + d + 16, 16)
         m = lax.rem(zz, 8) * 2 + lax.rem(c + f, 2)
-        low = g * ZC + (ZC // 2 if d == -4 else 0)
-        span = pl.ds(pl.multiple_of(low, 16), ZC // 2 if half else ZC)
+        span = pl.ds(pl.multiple_of(g * ZC, ZC), ZC)
         return remote(
             mixin.at[zz // 8, m // 4, lax.rem(m, 4), span],
             xm.at[zone, span],
@@ -224,40 +234,56 @@
             at_z(d, f),
         )
 
+    swapped(0).wait_recv()
+    relay(0).start()
+
     def step(g, carry):
         z0 = pl.multiple_of(g * ZC, ZC)
-        swapped(g).wait_recv()
-        relay(g).start()
+
+        @pl.when(g + 1 < NG)
+        def _():
+            swapped(g + 1).wait_recv()
+            relay(g + 1).start()
+
         onward(g).wait_recv()
         relay(g).wait_recv()
         for b in range(4):
-            block = st[b, :, pl.ds(z0, ZC), :].reshape(128, 512).astype(F32)
-            nrm[b * 128 : (b + 1) * 128, :] = rms(block, g_attn[...]).astype(BF16)
+            block = st[b, :, pl.ds(z0, ZC), :].reshape(R, 512).astype(F32)
+            nrm[b * R : (b + 1) * R, :] = rms(block, g_attn[...]).astype(BF16)
         for j in range(2):
             kv[:, j * 512 : (j + 1) * 512] = dot(
                 nrm[...], wq2[:, (j + 1) * 512 : (j + 2) * 512]
             ).astype(BF16)
-        qs[...] = dot(nrm[256:512, :], wq2[:, 0:512]).astype(BF16)
+        qs[...] = dot(nrm[2 * R :, :], wq2[:, 0:512]).astype(BF16)
+        pairs = [(t, hd) for t in range(2) for hd in range(HEADS)]
+        scores = []
+        for t, hd in pairs:
+            q = qs[t * R : (t + 1) * R, hd * HD : (hd + 1) * HD]
+            k = kv[t * R : (t + 3) * R, hd * HD : (hd + 1) * HD]
+            scores.append(
+                lax.dot_general(q, k, (((1,), (1,)), ((), ())), preferred_element_type=F32)
+            )
+        allowed = []
         for t in range(2):
-            gone = (col * 2 + t) >= 1
-            ok1 = jnp.where(gone, pats[t, 0:1, :], 0.0)
-            ok2 = jnp.where((col * 2 + t) >= 2, pats[t, 4:5, :], 0.0)
-            allowed = jnp.concatenate(
-                [same & (ok2 > 0.5), same & (ok1 > 0.5), causal], axis=1
-            )
-            for hd in range(HEADS):
-                q = qs[t * 128 : (t + 1) * 128, hd * HD : (hd + 1) * HD]
-                k = kv[t * 128 : t * 128 + 384, hd * HD : (hd + 1) * HD]
-                v = kv[t * 128 : t * 128 + 384, 512 + hd * HD : 512 + (hd + 1) * HD]
-                s = lax.dot_general(q, k, (((1,), (1,)), ((), ())), preferred_element_type=F32)
-                s = jnp.where(allowed, s * HD**-0.5, -1e30)
-                e = jnp.exp(s - jnp.max(s, axis=-1, keepdims=True))
-                total = jnp.sum(e, axis=-1, keepdims=True)
-                got = dot(e.astype(BF16), v) / total
-                ctx[t * 128 : (t + 1) * 128, hd * HD : (hd + 1) * HD] = got.astype(BF16)
+            ok1 = jnp.where((col * 2 + t) >= 1, pats[t, 0:1, 0 : 3 * R], 0.0) > 0.5
+            ok2 = jnp.where((col * 2 + t) >= 2, pats[t, 4:5, 0 : 3 * R], 0.0) > 0.5
+            allowed.append(causal | (back1 & ok1) | (back2 & ok2))
+        scores = [
+            jnp.where(allowed[t], s * HD**-0.5, -1e30) for (t, _), s in zip(pairs, scores)
+        ]
+        tops = [jnp.max(s, axis=-1, keepdims=True) for s in scores]
+        weights = [jnp.exp(s - top) for s, top in zip(scores, tops)]
+        got = [
+            dot(e.astype(BF16), kv[t * R : (t + 3) * R, 512 + hd * HD : 512 + (hd + 1) * HD])
+            for (t, hd), e in zip(pairs, weights)
+        ]
+        totals = [jnp.sum(e, axis=-1, keepdims=True) for e in weights]
+        for (t, hd), part, total in zip(pairs, got, totals):
+            ctx[t * R : (t + 1) * R, hd * HD : (hd + 1) * HD] = (part / total).astype(BF16)
+        both = dot(ctx[...], wa2[...])
         for t in range(2):
-            block = st[2 + t, :, pl.ds(z0, ZC), :].reshape(128, 512).astype(F32)
-            wide = block + dot(ctx[t * 128 : (t + 1) * 128, :], wa2[...])
+            block = st[2 + t, :, pl.ds(z0, ZC), :].reshape(R, 512).astype(F32)
+            wide = block + both[t * R : (t + 1) * R, :]
             aa[t] = wide
             mi = rms(wide, g_mix[...]).astype(BF16)
             for j in range(4):
@@ -272,36 +298,42 @@
 
     lax.fori_loop(0, NG, step, 0)
 
+    for n in (1, 2):
+        src, own = pieces[n]
+        pltpu.make_async_copy(src, own(zl), loc_sem.at[2 + n]).wait()
+        for k in range(7):
+            ag1(n, src, own, k).wait_recv()
     for k in range(15):
         ag2(1, own_i, k).start()
         ag2(2, own_o, k).start()
 
     locals_[1].wait()
-    for slot, (d, f, half) in enumerate(SLOTS):
-        span = pl.ds(0, 64 if half else 128)
-        remote(
-            mixin.at[0, 0, 0, span], xm.at[zone, span], fw_s.at[slot], fw_r.at[slot], other
-        ).wait()
+    for slot in range(len(SLOTS)):
+        remote(mixin.at[0, 0, 0], xm.at[zone], fw_s.at[slot], fw_r.at[slot], other).wait()
 
     def mixed(b):
         total = jnp.zeros((128, 128), F32)
         for k in range(3):
             weight = mx[b, k]
             live = jnp.where(k < degree[b], weight, jnp.zeros_like(weight))
-            total += dot(live, xm[neighbours[b, k]])
+            total += dot(live, xm[neighbours[k, b]])
         return total.astype(BF16)
 
+    def block_of(o):
+        return lax.rem(o // 8 + 1 + zone // 8, 2) * 8 + lax.rem(zone + o, 8)
+
     def back(o):
-        b = lax.rem(zone + o, 16)
+        b = block_of(o)
         return remote(stage.at[b], spat.at[zone], rt_s.at[o], rt_r.at[o], (tm, b))
 
     def send_back(o, carry):
-        b = lax.rem(zone + o, 16)
+        b = block_of(o)
         stage[b] = mixed(b)
         back(o).start()
         return carry
 
-    lax.fori_loop(1, 16, send_back, 0)
+    lax.fori_loop(0, 8, send_back, 0)
+    lax.fori_loop(9, 16, send_back, 0)
     spat[zone] = mixed(zone)
 
     for k in range(15):
@@ -331,9 +363,10 @@
     ag3(3, wo).wait()
 
     wi2, wo2 = wi.reshape(512, 2048), wo.reshape(2048, 512)
-    for o in range(1, 16):
-        back(o).wait()
-    for half in range(2):
+    for turn in range(2):
+        half = lax.rem(zone // 8 + turn, 2)
+        for o in range(0, 8) if turn else range(9, 16):
+            back(o).wait()
         for i in range(2):
             t = half * 2 + i
             wide = after[t] + jnp.concatenate(
@@ -346,38 +379,41 @@
                 dot(nf[...], wi2[:, j * 512 : (j + 1) * 512]), approximate=True
             ).astype(BF16)
             acc[...] += dot(hidden, wo2[j * 512 : (j + 1) * 512, :])
-        out[half * 2 : half * 2 + 2] = acc[...].astype(BF16).reshape(2, 128, 512)
+        out[pl.ds(half * 2, 2)] = acc[...].astype(BF16).reshape(2, 128, 512)
 
 
 def on_device(
     states, gain_attn, w_qkv, w_out_attn, pattern, gain_mix, neighbours, degree, mix, gain_ffn,
     w_in, w_out,
 ):
-    pat = jnp.broadcast_to(
-        jnp.repeat(pattern.reshape(2, 1).astype(F32), 4, axis=0), (8, 128)
-    )
     hbm = pl.BlockSpec(memory_space=pl.ANY)
     vmem = pl.BlockSpec(memory_space=pltpu.VMEM)
-    smem = pl.BlockSpec(memory_space=pltpu.SMEM)
     dma = pltpu.SemaphoreType.DMA
     return pl.pallas_call(
         kernel,
         out_shape=jax.ShapeDtypeStruct(states.shape, BF16),
-        in_specs=[hbm] * 6 + [vmem] * 4 + [smem] * 2,
+        in_specs=[hbm] * 12,
         out_specs=vmem,
         scratch_shapes=[
+            pltpu.VMEM((8, 256), F32),
+            pltpu.VMEM((1, 512), F32),
+            pltpu.VMEM((1, 512), F32),
+            pltpu.VMEM((1, 512), F32),
+            pltpu.SMEM((1, 2), jnp.int32),
+            pltpu.SMEM((3, 16), jnp.int32),
+            pltpu.SMEM((16,), jnp.int32),
             pltpu.VMEM((4, 4, 128, 512), BF16),
             pltpu.VMEM((8, 2, 2, 16, 1536), BF16),
             pltpu.VMEM((8, 2, 2, 16, 512), BF16),
             pltpu.VMEM((8, 2, 2, 16, 2048), BF16),
             pltpu.VMEM((8, 2, 8, 16, 512), BF16),
             pltpu.VMEM((16, 3, 128, 128), BF16),
-            pltpu.VMEM((2, 8, 128), F32),
-            pltpu.VMEM((512, 512), BF16),
-            pltpu.VMEM((512, 1024), BF16),
-            pltpu.VMEM((256, 512), BF16),
-            pltpu.VMEM((256, 512), BF16),
-            pltpu.VMEM((2, 128, 512), F32),
+            pltpu.VMEM((2, 8, 256), F32),
+            pltpu.VMEM((4 * R, 512), BF16),
+            pltpu.VMEM((4 * R, 1024), BF16),
+            pltpu.VMEM((2 * R, 512), BF16),
+            pltpu.VMEM((2 * R, 512), BF16),
+            pltpu.VMEM((2, R, 512), F32),
             pltpu.VMEM((4, 128, 512), F32),
             pltpu.VMEM((2, 4, 4, 128, 128), BF16),
             pltpu.VMEM((16, 128, 128), BF16),
@@ -385,7 +421,7 @@
             pltpu.VMEM((16, 128, 128), BF16),
             pltpu.VMEM((256, 512), BF16),
             pltpu.VMEM((256, 512), F32),
-            dma((6,)),
+            dma((12,)),
             dma((4, 7)), dma((4, 7)),
             dma((4, 15)), dma((4, 15)),
             dma((4,)), dma((4,)),
@@ -396,16 +432,16 @@
             dma((16,)), dma((16,)),
         ],
         compiler_params=pltpu.CompilerParams(
-            collective_id=0, has_side_effects=True, vmem_limit_bytes=48 << 20
+            collective_id=0, has_side_effects=True, vmem_limit_bytes=60 << 20
         ),
         cost_estimate=pl.CostEstimate(
             flops=5 * 10**9, bytes_accessed=8 * 10**6, transcendentals=2 * 10**6
         ),
         name="layer",
     )(
-        states, w_qkv, w_out_attn, w_in, w_out, mix, pat,
+        states, w_qkv, w_out_attn, w_in, w_out, mix,
         gain_attn.reshape(1, -1), gain_mix.reshape(1, -1), gain_ffn.reshape(1, -1),
-        neighbours, degree,
+        pattern, neighbours.T, degree,
     )
 
 

time: 150 us -> 129 us (0.86)
  Pallas kernels: 138 us -> 126 us
  local copies, waits for them, and re-layouts: 10.4 us -> 1.87 us
    pallas_call x1, Pallas kernels: 138 us -> 126 us  [on_device(): pl.pallas_call(kernel, out_shape=jax.ShapeDtypeStruct(states.shape, BF16)...]
    unnamed x22 -> x1, local copies, waits for them, and re-layouts: 10.2 us -> 1.87 us
where the time goes in v2:
time: 129 us; the launch traced here: 128 us
  Pallas kernels  126 us (98%)
  local copies, waits for them, and re-layouts  1.87 us (1%)
    pallas_call x1, Pallas kernels, on_device(): pl.pallas_call(kernel, out_shape=jax.ShapeDtypeStruct(states.shape, BF16)...  126 us

profile of v2, /device:TPU:1, one launch (start us, length us, event | category | flops | bytes accessed | tf_op | source)
XLA Modules:
  0.0 128.4 jit_solution(17410226092966492976)
XLA Ops:
  0.0 126.5 %layer.1 = bf16[4,128,512]{2,1,0:T(8,128)(2,1)} custom-call(bf16[4,128,512]{2,1,0:T(8,128)(2,1)} %states.1, bf16[32,1536]{1,0:T(8,128)(2,1)} %w_qkv.1, bf16[32,512]{1,0:T(8,128)(2,1)} %w_attn.1, bf16[32,2048]{1,0:T(8,128)(2,1)} %w_in.1, bf16[128,512]{1,0:T(8,128)(2,1)} %w_out.1, bf16[16,3,128,128]{3,2,1,0:T(8,128)(2,1)} %mix.1, f32[1,512]{1,0:T(1,128)} %bitcast.4, ...), custom_call_target="tpu_custom_call" | custom-call | flops 5000000000 | bytes 8000000 | tf_op jit(solution)/shard_map/layer/pallas_call | solution.py:392
  126.5 1.9 %copy.14 = bf16[4,128,512]{2,1,0:T(8,128)(2,1)} copy(bf16[4,128,512]{2,1,0:T(8,128)(2,1)} %layer.1) | data formatting | bytes 1048576

commit v3 on v2

--- a/solution.py
+++ b/solution.py
@@ -32,7 +32,7 @@
 def kernel(
     states, w_qkv, w_attn, w_in, w_out, mix, gains_a, gains_m, gains_f, pat_in, near_in, degree_in,
     out,
-    pat, g_attn, g_mix, g_ffn, pattern, neighbours, degree, st, wq, wa, wi, wo, mx, pats, nrm, kv, qs, ctx, aa, after, mixin, xm, stage, spat, nf, acc,
+    pat, g_attn, g_mix, g_ffn, pattern, neighbours, degree, st, wq, wa, wi, wo, mx, pats, nrm, kv, qs, ctx, aa, after, mixin, xm, stage, spat, nf, acc, result,
     loc_sem, ag1_s, ag1_r, ag2_s, ag2_r, ag3_s, ag3_r, e1_s, e1_r, ep_s, ep_r, e2_s, e2_r,
     fw_s, fw_r, rt_s, rt_r,
 ):
@@ -60,6 +60,13 @@
             src, dst, ssem, rsem, device_id=dev, device_id_type=MESH
         )
 
+    barrier = pltpu.get_barrier_semaphore()
+    for d in sorted(range(16), key=lambda v: -min(v, 16 - v)):
+        for f in (0, 1):
+            if (d, f) != (0, 0):
+                pl.semaphore_signal(barrier, inc=1, device_id=at_z(d, f), device_id_type=MESH)
+    for dx, dy in XY:
+        pl.semaphore_signal(barrier, inc=1, device_id=at_xy(dx, dy), device_id_type=MESH)
     locals_ = [
         pltpu.make_async_copy(states, st.at[2 + h], loc_sem.at[0]),
         pltpu.make_async_copy(mix, mx, loc_sem.at[1]),
@@ -114,13 +121,6 @@
     def _():
         pltpu.make_async_copy(src_a, own_a(zl), loc_sem.at[5]).start()
 
-    barrier = pltpu.get_barrier_semaphore()
-    for d in range(16):
-        for f in (0, 1):
-            if (d, f) != (0, 0):
-                pl.semaphore_signal(barrier, inc=1, device_id=at_z(d, f), device_id_type=MESH)
-    for dx, dy in XY:
-        pl.semaphore_signal(barrier, inc=1, device_id=at_xy(dx, dy), device_id_type=MESH)
     locals_[2].wait()
     upper = lax.broadcasted_iota(jnp.int32, (8, 256), 0) < 4
     pat[...] = jnp.where(upper, pattern[0, 0], pattern[0, 1]).astype(F32)
@@ -166,11 +166,16 @@
     send_pat.start()
     for g in range(NG):
         swap(g).start()
+        if g == 3:
+            for k in range(7):
+                ag1(1, src_i, own_i, k).start()
+                ag1(2, src_o, own_o, k).start()
         if g < 2:
             onward(g).start()
 
     def ag2(n, own, k):
-        return remote(own(every), own(every), ag2_s.at[n, k], ag2_r.at[n, k], at_xy(*XY[k]))
+        dev = at_xy((k + 1) // 4, lax.rem(k + 1, 4))
+        return remote(own(every), own(every), ag2_s.at[n, k], ag2_r.at[n, k], dev)
 
     for n in (0, 3):
         src, own = pieces[0] if n == 0 else (src_q, own_q)
@@ -192,9 +197,6 @@
 
     for g in range(2, NG):
         onward(g).start()
-    for k in range(7):
-        ag1(1, src_i, own_i, k).start()
-        ag1(2, src_o, own_o, k).start()
     for k in range(15):
         ag2(0, own_kv, k).wait_recv()
         ag2(3, own_q, k).wait_recv()
@@ -244,6 +246,17 @@
         def _():
             swapped(g + 1).wait_recv()
             relay(g + 1).start()
+
+        @pl.when(g == NG - 2)
+        def _():
+            for n in (1, 2):
+                src, own = pieces[n]
+                pltpu.make_async_copy(src, own(zl), loc_sem.at[2 + n]).wait()
+                for k in range(7):
+                    ag1(n, src, own, k).wait_recv()
+            for k in range(15):
+                ag2(1, own_i, k).start()
+                ag2(2, own_o, k).start()
 
         onward(g).wait_recv()
         relay(g).wait_recv()
@@ -298,15 +311,6 @@
 
     lax.fori_loop(0, NG, step, 0)
 
-    for n in (1, 2):
-        src, own = pieces[n]
-        pltpu.make_async_copy(src, own(zl), loc_sem.at[2 + n]).wait()
-        for k in range(7):
-            ag1(n, src, own, k).wait_recv()
-    for k in range(15):
-        ag2(1, own_i, k).start()
-        ag2(2, own_o, k).start()
-
     locals_[1].wait()
     for slot in range(len(SLOTS)):
         remote(mixin.at[0, 0, 0], xm.at[zone], fw_s.at[slot], fw_r.at[slot], other).wait()
@@ -363,6 +367,7 @@
     ag3(3, wo).wait()
 
     wi2, wo2 = wi.reshape(512, 2048), wo.reshape(2048, 512)
+    written = []
     for turn in range(2):
         half = lax.rem(zone // 8 + turn, 2)
         for o in range(0, 8) if turn else range(9, 16):
@@ -379,7 +384,15 @@
                 dot(nf[...], wi2[:, j * 512 : (j + 1) * 512]), approximate=True
             ).astype(BF16)
             acc[...] += dot(hidden, wo2[j * 512 : (j + 1) * 512, :])
-        out[pl.ds(half * 2, 2)] = acc[...].astype(BF16).reshape(2, 128, 512)
+        result[turn] = acc[...].astype(BF16).reshape(2, 128, 512)
+        written.append(
+            pltpu.make_async_copy(
+                result.at[turn], out.at[pl.ds(half * 2, 2)], loc_sem.at[turn]
+            )
+        )
+        written[turn].start()
+    for cp in written:
+        cp.wait()
 
 
 def on_device(
@@ -387,13 +400,12 @@
     w_in, w_out,
 ):
     hbm = pl.BlockSpec(memory_space=pl.ANY)
-    vmem = pl.BlockSpec(memory_space=pltpu.VMEM)
     dma = pltpu.SemaphoreType.DMA
     return pl.pallas_call(
         kernel,
         out_shape=jax.ShapeDtypeStruct(states.shape, BF16),
         in_specs=[hbm] * 12,
-        out_specs=vmem,
+        out_specs=hbm,
         scratch_shapes=[
             pltpu.VMEM((8, 256), F32),
             pltpu.VMEM((1, 512), F32),
@@ -421,6 +433,7 @@
             pltpu.VMEM((16, 128, 128), BF16),
             pltpu.VMEM((256, 512), BF16),
             pltpu.VMEM((256, 512), F32),
+            pltpu.VMEM((2, 2, 128, 512), BF16),
             dma((12,)),
             dma((4, 7)), dma((4, 7)),
             dma((4, 15)), dma((4, 15)),

time: 129 us -> 120 us (0.930)
  Pallas kernels: 126 us -> 118 us
    pallas_call x1, Pallas kernels: 126 us -> 118 us  [on_device(): pl.pallas_call(kernel, out_shape=jax.ShapeDtypeStruct(states.shape, BF16)...]
where the time goes in v3:
time: 120 us
  Pallas kernels  118 us (98%)
  local copies, waits for them, and re-layouts  1.87 us (2%)
    pallas_call x1, Pallas kernels, on_device(): pl.pallas_call(kernel, out_shape=jax.ShapeDtypeStruct(states.shape, BF16)...  118 us

profile of v3, /device:TPU:1, one launch (start us, length us, event | category | flops | bytes accessed | tf_op | source)
XLA Modules:
  0.0 119.9 jit_solution(17956655809960914563)
XLA Ops:
  0.0 118.0 %layer.1 = bf16[4,128,512]{2,1,0:T(8,128)(2,1)} custom-call(bf16[4,128,512]{2,1,0:T(8,128)(2,1)} %states.1, bf16[32,1536]{1,0:T(8,128)(2,1)} %w_qkv.1, bf16[32,512]{1,0:T(8,128)(2,1)} %w_attn.1, bf16[32,2048]{1,0:T(8,128)(2,1)} %w_in.1, bf16[128,512]{1,0:T(8,128)(2,1)} %w_out.1, bf16[16,3,128,128]{3,2,1,0:T(8,128)(2,1)} %mix.1, f32[1,512]{1,0:T(1,128)} %bitcast.4, ...), custom_call_target="tpu_custom_call" | custom-call | flops 5000000000 | bytes 8000000 | tf_op jit(solution)/shard_map/layer/pallas_call | solution.py:404
  118.0 1.9 %copy.14 = bf16[4,128,512]{2,1,0:T(8,128)(2,1)} copy(bf16[4,128,512]{2,1,0:T(8,128)(2,1)} %layer.1) | data formatting | bytes 1048576

commit v4 on v3

--- a/solution.py
+++ b/solution.py
@@ -13,6 +13,7 @@
 NG = 8
 ZC = 16
 R = 4 * ZC
+HELD = 6
 F32, BF16 = jnp.float32, jnp.bfloat16
 
 SLOTS = [(d, f) for d in (4, 3, -3, 2, -2, 1, -1, 0) for f in (0, 1) if (d, f) != (0, 0)]
@@ -150,6 +151,9 @@
         return remote(src, own(zl), ag1_s.at[n, k], ag1_r.at[n, k], at_z(RING[k], 0))
 
     send_pat = remote(pat, pats.at[h], ep_s, ep_r, partner)
+    send_pat.start()
+    swap(0).start()
+    onward(0).start()
     for k in range(7):
         ag1(0, src_kv, own_kv, k).start()
 
@@ -163,8 +167,7 @@
         for k in range(7):
             ag1(3, src_a, own_a, k).start()
 
-    send_pat.start()
-    for g in range(NG):
+    for g in range(1, NG):
         swap(g).start()
         if g == 3:
             for k in range(7):
@@ -221,13 +224,11 @@
     causal = same & (segment == 2) & (lax.rem(cols, R) // ZC <= rows // ZC)
     back1, back2 = same & (segment == 1), same & (segment == 0)
 
-    def fw(slot, g):
-        d, f = SLOTS[slot]
-        if d == 4:
-            d = 4 - 8 * lax.rem(g, 2)
+    def fw(slot, d, low, count):
+        f = SLOTS[slot][1]
         zz = lax.rem(z + d + 16, 16)
         m = lax.rem(zz, 8) * 2 + lax.rem(c + f, 2)
-        span = pl.ds(pl.multiple_of(g * ZC, ZC), ZC)
+        span = pl.ds(low, count)
         return remote(
             mixin.at[zz // 8, m // 4, lax.rem(m, 4), span],
             xm.at[zone, span],
@@ -236,6 +237,19 @@
             at_z(d, f),
         )
 
+    def send_held():
+        for slot, (d, f) in enumerate(SLOTS):
+            if d == 4:
+                fw(slot, 4, 0, HELD * ZC // 2).start()
+                fw(slot, -4, HELD * ZC // 2, HELD * ZC // 2).start()
+            else:
+                fw(slot, d, 0, HELD * ZC).start()
+
+    def send_chunk(g):
+        for slot, (d, f) in enumerate(SLOTS):
+            way = 4 - 8 * lax.rem(g, 2) if d == 4 else d
+            fw(slot, way, pl.multiple_of(g * ZC, ZC), ZC).start()
+
     swapped(0).wait_recv()
     relay(0).start()
 
@@ -246,6 +260,10 @@
         def _():
             swapped(g + 1).wait_recv()
             relay(g + 1).start()
+
+        @pl.when(g == HELD)
+        def _():
+            send_held()
 
         @pl.when(g == NG - 2)
         def _():
@@ -303,8 +321,10 @@
                 mixin[t, :, j, pl.ds(z0, ZC), :] = mi[:, j * 128 : (j + 1) * 128].reshape(
                     4, ZC, 128
                 )
-        for slot in range(len(SLOTS)):
-            fw(slot, g).start()
+        @pl.when(g >= HELD)
+        def _():
+            send_chunk(g)
+
         after[:, pl.ds(z0, ZC), :] = aa[h].reshape(4, ZC, 512)
         xm[zone, pl.ds(z0, ZC), :] = mixin[h, zone // 4, lax.rem(zone, 4), pl.ds(z0, ZC), :]
         return carry

time: 120 us -> 119 us (level)
  Pallas kernels: 118 us -> 116 us
    pallas_call x1, Pallas kernels: 118 us -> 116 us  [on_device(): pl.pallas_call(kernel, out_shape=jax.ShapeDtypeStruct(states.shape, BF16)...]
where the time goes in v4:
time: 119 us; the launch traced here: 118 us
  Pallas kernels  116 us (97%)
  local copies, waits for them, and re-layouts  1.87 us (2%)
    pallas_call x1, Pallas kernels, on_device(): pl.pallas_call(kernel, out_shape=jax.ShapeDtypeStruct(states.shape, BF16)...  116 us

profile of v4, /device:TPU:1, one launch (start us, length us, event | category | flops | bytes accessed | tf_op | source)
XLA Modules:
  0.0 118.4 jit_solution(15649713901561253363)
XLA Ops:
  0.0 116.5 %layer.1 = bf16[4,128,512]{2,1,0:T(8,128)(2,1)} custom-call(bf16[4,128,512]{2,1,0:T(8,128)(2,1)} %states.1, bf16[32,1536]{1,0:T(8,128)(2,1)} %w_qkv.1, bf16[32,512]{1,0:T(8,128)(2,1)} %w_attn.1, bf16[32,2048]{1,0:T(8,128)(2,1)} %w_in.1, bf16[128,512]{1,0:T(8,128)(2,1)} %w_out.1, bf16[16,3,128,128]{3,2,1,0:T(8,128)(2,1)} %mix.1, f32[1,512]{1,0:T(1,128)} %bitcast.4, ...), custom_call_target="tpu_custom_call" | custom-call | flops 5000000000 | bytes 8000000 | tf_op jit(solution)/shard_map/layer/pallas_call | solution.py:424
  116.5 1.9 %copy.14 = bf16[4,128,512]{2,1,0:T(8,128)(2,1)} copy(bf16[4,128,512]{2,1,0:T(8,128)(2,1)} %layer.1) | data formatting | bytes 1048576

commit v5 on v4

--- a/solution.py
+++ b/solution.py
@@ -185,8 +185,9 @@
         pltpu.make_async_copy(src, own(zl), loc_sem.at[2 if n == 0 else 5]).wait()
         for k in range(7):
             ag1(n, src, own, k).wait_recv()
-    for k in range(15):
-        ag2(0, own_kv, k).start()
+        if n == 0:
+            for k in range(15):
+                ag2(0, own_kv, k).start()
 
     @pl.when(first)
     def _():
@@ -209,6 +210,8 @@
 
     ag3(0, wq).start()
     ag3(1, wa).start()
+    swapped(0).wait_recv()
+    relay(0).start()
     locals_[0].wait()
     for n in (3, 4, 5, 6, 7):
         locals_[n].wait()
@@ -250,8 +253,6 @@
             way = 4 - 8 * lax.rem(g, 2) if d == 4 else d
             fw(slot, way, pl.multiple_of(g * ZC, ZC), ZC).start()
 
-    swapped(0).wait_recv()
-    relay(0).start()
 
     def step(g, carry):
         z0 = pl.multiple_of(g * ZC, ZC)

time: 119 us -> 119 us (level)
  no operation moved by 1% of the time
where the time goes in v5:
time: 119 us; the launch traced here: 118 us
  Pallas kernels  116 us (97%)
  local copies, waits for them, and re-layouts  1.87 us (2%)
    pallas_call x1, Pallas kernels, on_device(): pl.pallas_call(kernel, out_shape=jax.ShapeDtypeStruct(states.shape, BF16)...  116 us

profile of v5, /device:TPU:1, one launch (start us, length us, event | category | flops | bytes accessed | tf_op | source)
XLA Modules:
  0.0 118.1 jit_solution(7551196994791476430)
XLA Ops:
  0.0 116.2 %layer.1 = bf16[4,128,512]{2,1,0:T(8,128)(2,1)} custom-call(bf16[4,128,512]{2,1,0:T(8,128)(2,1)} %states.1, bf16[32,1536]{1,0:T(8,128)(2,1)} %w_qkv.1, bf16[32,512]{1,0:T(8,128)(2,1)} %w_attn.1, bf16[32,2048]{1,0:T(8,128)(2,1)} %w_in.1, bf16[128,512]{1,0:T(8,128)(2,1)} %w_out.1, bf16[16,3,128,128]{3,2,1,0:T(8,128)(2,1)} %mix.1, f32[1,512]{1,0:T(1,128)} %bitcast.4, ...), custom_call_target="tpu_custom_call" | custom-call | flops 5000000000 | bytes 8000000 | tf_op jit(solution)/shard_map/layer/pallas_call | solution.py:425
  116.2 1.9 %copy.14 = bf16[4,128,512]{2,1,0:T(8,128)(2,1)} copy(bf16[4,128,512]{2,1,0:T(8,128)(2,1)} %layer.1) | data formatting | bytes 1048576
